TPU v7x, 512 devices: a whole 4x8x8 slice. The times are simulated.
512 devices in a mesh: island: 16 (over y_hi, x), mp: 32 (over y_lo, z, core).
Axes of the slice: x: 4, y: 8 (y_hi: 4, y_lo: 2; y = y_hi * 2 + y_lo), z: 8, core: 2. Of those that a mesh axis runs over, the one named last changes fastest.
Arguments:
- global_params: bfloat16 [512, 12288], P(None, 'mp'), may hold values from -4 to 4
- local_params: bfloat16 [8192, 12288], P('island', 'mp'), may hold values from -16 to 16
- residual: bfloat16 [8192, 12288], P('island', 'mp'), may hold values from -4 to 4
- momentum: float32 [512, 12288], P('island', 'mp'), may hold values from -3 to 3
- kept: int32 [16, 16], replicated, may hold values from 1 to 4, as said below
- owner: int32 [64], replicated, may hold values from 0 to 15, as said below
- queries: bfloat16 [16384, 12288], P('island', 'mp'), may hold values from -6 to 6
- keys: bfloat16 [16384, 12288], P('island', 'mp'), may hold values from -6 to 6
- values: bfloat16 [16384, 12288], P('island', 'mp'), may hold values from -6 to 6
Outputs:
- merged: bfloat16 [512, 12288], P(None, 'mp')
- new_residual: bfloat16 [8192, 12288], P('island', 'mp')
- new_momentum: float32 [512, 12288], P('island', 'mp')
- attended: bfloat16 [16384, 12288], P('island', 'mp')
Inputs may be any that keep to these rules, and one draw needn't show every extreme that they name: Island i sends the first kept[i, o] (in block order) of the blocks owned by island o; some owner receives 4 blocks from every island. `owner`: every island owns exactly 4 row blocks.
All inputs are finite; a program needn't handle non-finite values.
Results may differ from a plain program's by a relative error of at most 0.015.
Values may be sent and summed in bfloat16 or wider, within the bound.
No kernel may reach another device: no remote copies, remote signals or barrier semaphores. Data moves between devices by JAX's collectives and lax.ppermute only.
A program may use at most 64 MiB of HBM per device.

v0:
```python
import math

import jax
import jax.numpy as jnp
from jax import lax
from jax.sharding import PartitionSpec as P

D = 12288
HEAD = 128


clip_level = 1.4
momentum_rate = 0.9
outer_rate = 0.7
epsilon = 1e-06


def attend(queries, keys, values):
    seq_rows = queries.shape[0]
    heads = queries.shape[1] // HEAD
    step_rows = min(512, seq_rows)
    key_heads = keys.reshape(seq_rows, heads, HEAD)
    value_heads = values.reshape(seq_rows, heads, HEAD)
    scale = 1.0 / math.sqrt(HEAD)
    pieces = []
    for begin in range(0, seq_rows, step_rows):
        query_block = queries[begin : begin + step_rows].reshape(step_rows, heads, HEAD)
        scores = (
            jnp.einsum("qhd,khd->hqk", query_block, key_heads, preferred_element_type=jnp.float32)
            * scale
        )
        causal = (begin + jnp.arange(step_rows))[:, None] >= jnp.arange(seq_rows)[None, :]
        scores = jnp.where(causal[None], scores, -jnp.inf)
        top = jnp.max(scores, axis=-1, keepdims=True)
        expo = jnp.exp(scores - top)
        probs = (expo / jnp.sum(expo, axis=-1, keepdims=True)).astype(jnp.bfloat16)
        mixed = jnp.einsum("hqk,khd->qhd", probs, value_heads, preferred_element_type=jnp.float32)
        pieces.append(mixed.astype(jnp.bfloat16).reshape(step_rows, heads * HEAD))
    return jnp.concatenate(pieces, axis=0)


def local(global_params, local_params, residual, momentum, kept, owner, queries, keys, values):
    f32 = jnp.float32
    islands = lax.axis_size("island")
    myself = lax.axis_index("island")
    columns = global_params.shape[1]
    blocks = owner.shape[0]
    block_rows = global_params.shape[0] // blocks
    own_blocks = blocks // islands
    own_rows = own_blocks * block_rows
    combined = global_params.astype(f32) - local_params.astype(f32) + residual.astype(f32)
    index = jnp.arange(blocks, dtype=jnp.int32)
    same = owner[None, :] == owner[:, None]
    slot_of = jnp.sum((same & (index[None, :] < index[:, None])).astype(jnp.int32), axis=1)
    packed_pos = owner * own_blocks + slot_of
    inverse = jnp.sum(jnp.where(packed_pos[None, :] == index[:, None], index[None, :], 0), axis=1)
    my_counts = lax.dynamic_index_in_dim(kept, myself, 0, keepdims=False)
    owner_table = owner[:, None] == jnp.arange(islands, dtype=jnp.int32)[None, :]
    limit = jnp.sum(jnp.where(owner_table, my_counts[None, :], 0), axis=1)
    row_mask = jnp.repeat(slot_of < limit, block_rows)[:, None]
    sent = jnp.where(row_mask, combined.astype(jnp.bfloat16), jnp.zeros((), jnp.bfloat16))
    new_residual = jnp.where(row_mask, combined - sent.astype(f32), combined).astype(jnp.bfloat16)
    outgoing = sent.reshape(blocks, block_rows, columns)[inverse]
    received = lax.all_to_all(
        outgoing.reshape(islands, own_rows, columns),
        "island",
        split_axis=0,
        concat_axis=0,
        tiled=True,
    )
    average = jnp.sum(received.astype(f32), axis=0) / islands
    blockwise = average.reshape(own_blocks, block_rows * columns)
    partial_square = jnp.sum(blockwise * blockwise, axis=1)
    total_square = lax.psum(partial_square, "mp")
    root = jnp.sqrt(total_square / (block_rows * D) + epsilon)
    factor = jnp.minimum(1.0, clip_level / math.sqrt(islands) / root)
    clipped = average * jnp.repeat(factor, block_rows)[:, None]
    new_moment = momentum_rate * momentum + clipped
    update = clipped + momentum_rate * new_moment
    my_blocks = lax.dynamic_slice_in_dim(inverse, myself * own_blocks, own_blocks)
    my_global = global_params.reshape(blocks, block_rows, columns)[my_blocks].reshape(
        own_rows, columns
    )
    fresh = (my_global.astype(f32) - outer_rate * update).astype(jnp.bfloat16)
    attended = attend(queries, keys, values)
    everything = lax.all_gather(fresh, "island", axis=0, tiled=True)
    merged = everything.reshape(blocks, block_rows, columns)[packed_pos].reshape(
        blocks * block_rows, columns
    )
    return (merged, new_residual, new_moment, attended)


def solution(mesh):
    placed = (
        P(None, "mp"),
        P("island", "mp"),
        P("island", "mp"),
        P("island", "mp"),
        P(),
        P(),
        P("island", "mp"),
        P("island", "mp"),
        P("island", "mp"),
    )
    return jax.shard_map(
        local,
        mesh=mesh,
        in_specs=placed,
        out_specs=(P(None, "mp"), P("island", "mp"), P("island", "mp"), P("island", "mp")),
        check_vma=False,
    )
```

profile of v0, /device:TPU:8, one launch (start us, length us, event | category | flops | bytes accessed | tf_op | source)
XLA Modules:
  0.0 151.6 jit_solution(5920383587640348071)
XLA Ops:
  0.6 0.0 copy-start
  0.6 0.0 copy-start.4
  0.7 0.0 copy-start.5
  0.7 1.0 convert_reduce_fusion.1
  1.6 1.2 compare_select_fusion
  2.8 0.1 select_reduce_fusion
  3.0 0.0 copy-start.8
  3.0 0.0 copy-done
  3.0 0.7 select_reduce_fusion.1
  3.7 0.1 broadcast_in_dim.100
  3.8 0.1 broadcast_in_dim.101
  4.0 1.4 fusion.21
  5.4 1.4 gather_fusion.1
  6.7 8.8 %all-to-all-start = ((bf16[16,32,384]{2,1,0:T(8,128)(2,1)}), bf16[16,32,384]{2,1,0:T(8,128)(2,1)S(1)}, u32[]{:S(2)}, u32[]{:S(2)}) async-start(bf16[16,32,384]{2,1,0:T(8,128)(2,1)} %bitcast.6), calls=%async_computation | async-start | bytes 786432 | tf_op jit(solution)/shard_map/all_to_all | solution.py:64
  15.5 0.9 iota_compare_fusion.1
  16.5 1.2 fusion.29
  17.7 0.9 copy.43
  18.6 0.3 copy.30
  18.9 0.3 copy.33
  19.2 0.2 copy.44
  19.4 0.4 iota_compare_fusion
  19.8 6.2 %fusion.31 = (f32[3,512]{1,0:T(4,128)S(1)}, f32[3,512,1024]{2,1,0:T(8,128)}) fusion(pred[512,1024]{1,0:T(8,128)(4,1)} %iota_compare_fusion.1, bf16[512,3,128]{0,2,1:T(8,128)(2,1)} %bitcast.43, bf16[1024,3,128]{0,2,1:T(8,128)(2,1)S(1)} %bitcast.39), kind=kOutput, calls=%fused_computation.63 | convolution fusion | flops 408945664 | bytes 8001536 | tf_op jit(solution)/shard_map/sub | solution.py:35
  26.0 5.6 %fusion.30 = (f32[3,512]{1,0:T(4,128)}, f32[3,512,1024]{2,1,0:T(8,128)}) fusion(pred[512,1024]{1,0:T(8,128)(4,1)S(1)} %iota_compare_fusion, bf16[512,3,128]{0,2,1:T(8,128)(2,1)S(1)} %bitcast.44, bf16[1024,3,128]{0,2,1:T(8,128)(2,1)S(1)} %bitcast.40), kind=kOutput, calls=%fused_computation.62 | convolution fusion | flops 408945664 | bytes 8001536 | tf_op jit(solution)/shard_map/sub | solution.py:35
  31.6 4.2 %fusion.13 = bf16[3,512,128]{1,2,0:T(8,128)(2,1)S(1)} fusion(bf16[1024,3,128]{0,2,1:T(8,128)(2,1)S(1)} %bitcast.37, f32[3,512,1024]{2,1,0:T(8,128)} %get-tuple-element.13, f32[3,512]{1,0:T(4,128)S(1)} %get-tuple-element.12), kind=kOutput, calls=%fused_computation.24 | convolution fusion | flops 405995520 | bytes 7477248 | tf_op jit(solution)/shard_map/hqk,khd->qhd/dot_general | solution.py:37
  35.8 0.4 copy-done.10
  36.2 0.0 copy-start.2
  36.2 0.0 copy-start.3
  36.2 0.0 copy-start.6
  36.2 1.3 fusion.12
  37.5 0.2 copy.37
  37.7 0.2 copy.38
  38.0 0.1 compare_select_fusion.2
  38.1 1.0 pad_maximum_fusion
  39.0 0.0 copy-done.1
  39.0 0.0 copy-done.3
  39.0 1.0 fusion.14
  40.0 0.0 all-to-all-done
  40.0 0.1 convert_reduce_fusion
  40.1 0.1 multiply_reduce_fusion
  40.2 0.1 reduce_sum.78
  40.3 0.1 reduce_sum.79
  40.4 0.6 gather_fusion
  41.0 62.0 %psum.7 = f32[4]{0:T(128)S(1)} all-reduce(f32[4]{0:T(128)S(1)} %reduce_sum.79), channel_id=1, replica_groups=mesh['island'=16,'mp'=32] {'mp'}, use_global_device_ids=true, to_apply=%region_6.7 | all-reduce | flops 4 | bytes 32 | tf_op jit(solution)/shard_map/psum | solution.py:74
  103.0 0.1 broadcast_in_dim.104
  103.0 0.1 mul.51
  103.1 0.7 fusion.22
  103.8 46.4 %all_gather.3 = bf16[512,384]{1,0:T(8,128)(2,1)S(1)} all-gather(bf16[32,384]{1,0:T(8,128)(2,1)S(1)} %get-tuple-element.6), channel_id=1, replica_groups=mesh['island'=16,'mp'=32] {'island'}, dimensions={0}, use_global_device_ids=true | all-gather | bytes 417792 | tf_op jit(solution)/shard_map/all_gather | solution.py:86
  150.2 1.4 gather_fusion.2
  (21 shorter events, 0.1 us)
Async XLA Ops:
  0.6 2.3 %copy-start = (s32[16,16]{1,0:T(8,128)S(1)}, s32[16,16]{1,0:T(8,128)}, u32[]{:S(2)}) copy-start(s32[16,16]{1,0:T(8,128)} %param.13) | copy-start | bytes 3076
  0.6 18.0 %copy-start.4 = (bf16[1024,384]{1,0:T(8,128)(2,1)S(1)}, bf16[1024,384]{1,0:T(8,128)(2,1)}, u32[]{:S(2)}) copy-start(bf16[1024,384]{1,0:T(8,128)(2,1)} %param.16) | copy-start | bytes 2359300
  0.7 18.3 %copy-start.5 = (bf16[1024,384]{1,0:T(8,128)(2,1)S(1)}, bf16[1024,384]{1,0:T(8,128)(2,1)}, u32[]{:S(2)}) copy-start(bf16[1024,384]{1,0:T(8,128)(2,1)} %param.17) | copy-start | bytes 2359300
  3.0 14.7 %copy-start.8 = (s32[64]{0:T(128)}, s32[64]{0:T(128)S(1)}, u32[]{:S(2)}) copy-start(s32[64]{0:T(128)S(1)} %select_reduce_fusion) | copy-start | bytes 772
  6.7 33.3 %all-to-all-start = ((bf16[16,32,384]{2,1,0:T(8,128)(2,1)}), bf16[16,32,384]{2,1,0:T(8,128)(2,1)S(1)}, u32[]{:S(2)}, u32[]{:S(2)}) async-start(bf16[16,32,384]{2,1,0:T(8,128)(2,1)} %bitcast.6), calls=%async_computation | async-start | bytes 786432 | tf_op jit(solution)/shard_map/all_to_all | solution.py:64
  31.6 4.6 %copy-start.10 = (f32[3,512,1024]{2,1,0:T(8,128)S(1)}, f32[3,512,1024]{2,1,0:T(8,128)}, u32[]{:S(2)}) copy-start(f32[3,512,1024]{2,1,0:T(8,128)} %get-tuple-element.11) | copy-start | bytes 18874372
  31.6 4.6 %copy-start.11 = (f32[3,512]{1,0:T(4,128)S(1)}, f32[3,512]{1,0:T(4,128)}, u32[]{:S(2)}) copy-start(f32[3,512]{1,0:T(4,128)} %get-tuple-element.10) | copy-start | bytes 18436
  36.2 1.8 %copy-start.9 = (s32[64]{0:T(128)S(1)}, s32[64]{0:T(128)}, u32[]{:S(2)}) copy-start(s32[64]{0:T(128)} %copy-done.8) | copy-start | bytes 772
  36.2 1.9 %copy-start.7 = (s32[64]{0:T(128)S(1)}, s32[64]{0:T(128)}, u32[]{:S(2)}) copy-start(s32[64]{0:T(128)} %get-tuple-element.4) | copy-start | bytes 772
  36.2 2.9 %copy-start.1 = (bf16[512,384]{1,0:T(8,128)(2,1)S(1)}, bf16[512,384]{1,0:T(8,128)(2,1)}, u32[]{:S(2)}) copy-start(bf16[512,384]{1,0:T(8,128)(2,1)} %param.9) | copy-start | bytes 1179652
  36.2 2.9 %copy-start.2 = (bf16[512,384]{1,0:T(8,128)(2,1)S(1)}, bf16[512,384]{1,0:T(8,128)(2,1)}, u32[]{:S(2)}) copy-start(bf16[512,384]{1,0:T(8,128)(2,1)} %param.11) | copy-start | bytes 1179652
  36.2 2.9 %copy-start.3 = (bf16[512,384]{1,0:T(8,128)(2,1)S(1)}, bf16[512,384]{1,0:T(8,128)(2,1)}, u32[]{:S(2)}) copy-start(bf16[512,384]{1,0:T(8,128)(2,1)} %param.10) | copy-start | bytes 1179652
  36.2 66.9 %copy-start.6 = (f32[32,384]{1,0:T(8,128)S(1)}, f32[32,384]{1,0:T(8,128)}, u32[]{:S(2)}) copy-start(f32[32,384]{1,0:T(8,128)} %param.12) | copy-start | bytes 147460
where the time goes:
time: 152 us
  blocking collectives  108 us (71%)
  matrix products  17.3 us (11%)
  other arithmetic  8.8 us (6%)
  starting transfers between devices  8.77 us (6%)
  local copies, waits for them, and re-layouts  7.53 us (5%)
    psum x1, blocking collectives, local(): total_square = lax.psum(partial_square, 'mp')  62 us
    all_gather x1, blocking collectives, local(): everything = lax.all_gather(fresh, 'island', axis=0, tiled=True)  46.4 us
    sub x2, matrix products, attend(): expo = jnp.exp(scores - top)  11.8 us
    all_to_all x1, starting transfers between devices, local(): lax.all_to_all(outgoing.reshape(islands, own_rows, columns), 'island', sp...  8.77 us
    dot_general x2, matrix products, attend(): jnp.einsum('hqk,khd->qhd', probs, value_heads, preferred_element_type=jnp...  5.51 us
  transfers between devices with their start and end apart: 1, of which 0 were waited for; matrix products, arithmetic and copies ran while one was open for 16% of the time, Pallas kernels for 0%

commit v1 on v0

v1 whole, which is shorter than its diff:
```python
import functools
import math

import jax
import jax.numpy as jnp
from jax import lax
from jax.experimental import pallas as pl
from jax.experimental.pallas import tpu as pltpu
from jax.sharding import PartitionSpec as P

D = 12288
HEAD = 128

clip_level = 1.4
momentum_rate = 0.9
outer_rate = 0.7
epsilon = 1e-06

f32 = jnp.float32
bf16 = jnp.bfloat16
i32 = jnp.int32


def iota(shape, axis):
    return lax.broadcasted_iota(i32, shape, axis)


def places(owner_row, own_blocks):
    blocks = owner_row.shape[1]
    sub, lane = iota((blocks, blocks), 0), iota((blocks, blocks), 1)
    owner_col = jnp.sum(jnp.where(sub == lane, owner_row, 0), axis=1, keepdims=True)
    before = (owner_col == owner_row) & (lane < sub)
    slot_col = jnp.sum(before.astype(i32), axis=1, keepdims=True)
    return owner_col, slot_col, owner_col * own_blocks + slot_col


def sent_blocks(owner_col, slot_col, kept, me):
    islands = kept.shape[0]
    mine = jnp.sum(jnp.where(iota(kept.shape, 0) == me, kept, 0), axis=0, keepdims=True)
    shape = (owner_col.shape[0], islands)
    limit = jnp.sum(jnp.where(iota(shape, 1) == owner_col, mine, 0), axis=1, keepdims=True)
    return slot_col < limit


def spread_lanes(col, rows, block_rows):
    shape = (col.shape[0], rows)
    return jnp.sum(
        jnp.where(iota(shape, 1) // block_rows == iota(shape, 0), col, 0), axis=0, keepdims=True
    )


def spread_rows(col, rows, block_rows):
    blocks = col.shape[0]
    square = (blocks, blocks)
    row = jnp.sum(jnp.where(iota(square, 0) == iota(square, 1), col, 0), axis=0, keepdims=True)
    shape = (rows, blocks)
    return jnp.sum(
        jnp.where(iota(shape, 0) // block_rows == iota(shape, 1), row, 0), axis=1, keepdims=True
    )


def pack_kernel(block_rows, own_blocks, me_ref, owner_ref, kept_ref, global_ref, local_ref, residual_ref, out_ref):
    rows = global_ref.shape[0]
    owner_col, slot_col, packed_col = places(owner_ref[...], own_blocks)
    sent = sent_blocks(owner_col, slot_col, kept_ref[...], me_ref[0])
    goal = spread_lanes(jnp.where(sent, packed_col * block_rows, -rows), rows, block_rows)
    goal = goal + iota((1, rows), 1) % block_rows
    table = jnp.where(iota((rows, rows), 0) == goal, 1.0, 0.0).astype(bf16)
    combined = global_ref[...].astype(f32) - local_ref[...].astype(f32) + residual_ref[...].astype(f32)
    out_ref[...] = jnp.dot(table, combined.astype(bf16), preferred_element_type=f32).astype(bf16)


def side_kernel(block_rows, own_blocks, me_ref, owner_ref, kept_ref, global_ref, local_ref, residual_ref, new_ref, table_ref, mine_ref):
    rows = global_ref.shape[0]
    me = me_ref[0]
    owner_col, slot_col, packed_col = places(owner_ref[...], own_blocks)
    sent = sent_blocks(owner_col, slot_col, kept_ref[...], me)
    mask = spread_rows(sent.astype(i32), rows, block_rows) > 0
    fragment = global_ref[...]
    combined = fragment.astype(f32) - local_ref[...].astype(f32) + residual_ref[...].astype(f32)
    kept_part = jnp.where(mask, combined.astype(bf16).astype(f32), 0.0)
    new_ref[...] = (combined - kept_part).astype(bf16)
    goal = spread_rows(packed_col * block_rows, rows, block_rows)
    goal = goal + iota((rows, 1), 0) % block_rows
    table_ref[...] = jnp.where(iota((rows, rows), 1) == goal, 1.0, 0.0).astype(bf16)
    own_rows = own_blocks * block_rows
    place = spread_lanes(packed_col * block_rows, rows, block_rows) + iota((1, rows), 1) % block_rows
    pick = jnp.where(iota((own_rows, rows), 0) + me * own_rows == place, 1.0, 0.0).astype(bf16)
    mine_ref[...] = jnp.dot(pick, fragment, preferred_element_type=f32).astype(bf16)


def average_kernel(block_rows, received_ref, average_ref, square_ref):
    islands, own_rows, _ = received_ref.shape
    average = jnp.sum(received_ref[...].astype(f32), axis=0) / islands
    average_ref[...] = average
    squares = average * average
    lane = iota((1, 128), 1)
    row = jnp.zeros((1, 128), f32)
    for block in range(own_rows // block_rows):
        part = squares[block * block_rows : (block + 1) * block_rows]
        total = jnp.sum(jnp.sum(part, axis=0, keepdims=True), axis=1, keepdims=True)
        row = jnp.where(lane == block, total, row)
    square_ref[...] = jnp.broadcast_to(row, square_ref.shape)


def update_kernel(block_rows, islands, square_ref, average_ref, momentum_ref, mine_ref, moment_ref, fresh_ref):
    own_rows = average_ref.shape[0]
    total = jnp.sum(square_ref[...], axis=0, keepdims=True)
    root = jnp.sqrt(total / (block_rows * D) + epsilon)
    factor = jnp.minimum(1.0, clip_level / math.sqrt(islands) / root)
    lane = iota((1, 128), 1)
    for block in range(own_rows // block_rows):
        part = pl.ds(block * block_rows, block_rows)
        scale = jnp.sum(jnp.where(lane == block, factor, 0.0), axis=1, keepdims=True)
        clipped = average_ref[part, :] * scale
        moment_ref[part, :] = momentum_rate * momentum_ref[part, :] + clipped
    scales = jnp.concatenate(
        [
            jnp.broadcast_to(
                jnp.sum(jnp.where(lane == block, factor, 0.0), axis=1, keepdims=True), (block_rows, 1)
            )
            for block in range(own_rows // block_rows)
        ],
        axis=0,
    )
    update = average_ref[...] * scales + momentum_rate * moment_ref[...]
    fresh = (mine_ref[...].astype(f32) - outer_rate * update).astype(bf16)
    for island in range(islands):
        fresh_ref[island] = fresh


def merge_kernel(table_ref, fresh_ref, out_ref):
    islands, own_rows, columns = fresh_ref.shape
    fresh = fresh_ref[...].reshape(islands * own_rows, columns)
    out_ref[...] = jnp.dot(table_ref[...], fresh, preferred_element_type=f32).astype(bf16)


def attend_kernel(step, query_ref, key_ref, value_ref, out_ref):
    rows = query_ref.shape[0]
    rate = math.log2(math.e) / math.sqrt(HEAD)
    values = jnp.concatenate([value_ref[...], jnp.ones((rows, HEAD), bf16)], axis=1)
    lower = iota((step, step), 0) >= iota((step, step), 1)
    for begin in range(0, rows, step):
        end = begin + step
        query = query_ref[begin:end, :]
        across = (((1,), (1,)), ((), ()))
        corner = lax.dot_general(query, key_ref[begin:end, :], across, preferred_element_type=f32)
        corner = jnp.where(lower, corner, -jnp.inf)
        top = jnp.max(corner, axis=1, keepdims=True)
        if begin:
            past = lax.dot_general(query, key_ref[:begin, :], across, preferred_element_type=f32)
            top = jnp.maximum(top, jnp.max(past, axis=1, keepdims=True))
        expo = jnp.exp2((corner - top) * rate).astype(bf16)
        mixed = jnp.dot(expo, values[begin:end], preferred_element_type=f32)
        if begin:
            expo = jnp.exp2((past - top) * rate).astype(bf16)
            mixed = mixed + jnp.dot(expo, values[:begin], preferred_element_type=f32)
        out_ref[begin:end, :] = (mixed[:, :HEAD] / mixed[:, HEAD : HEAD + 1]).astype(bf16)


def attend(queries, keys, values):
    rows, columns = queries.shape
    heads = columns // HEAD
    head = pl.BlockSpec((rows, HEAD), lambda h: (0, h))
    return pl.pallas_call(
        functools.partial(attend_kernel, 256),
        grid=(heads,),
        in_specs=[head] * 3,
        out_specs=head,
        out_shape=jax.ShapeDtypeStruct(queries.shape, bf16),
        compiler_params=pltpu.CompilerParams(vmem_limit_bytes=32 << 20),
        cost_estimate=pl.CostEstimate(
            flops=3 * rows * rows * columns,
            bytes_accessed=8 * rows * columns,
            transcendentals=rows * rows * heads // 2,
        ),
        name="attend",
    )(queries, keys, values)


def call(body, out_shape, name, smem=0, flops=0):
    vmem = pl.BlockSpec(memory_space=pltpu.VMEM)

    def run(*args):
        return pl.pallas_call(
            body,
            in_specs=[pl.BlockSpec(memory_space=pltpu.SMEM)] * smem + [vmem] * (len(args) - smem),
            out_specs=jax.tree.map(lambda _: vmem, out_shape),
            out_shape=out_shape,
            compiler_params=pltpu.CompilerParams(vmem_limit_bytes=32 << 20),
            cost_estimate=pl.CostEstimate(flops=flops, bytes_accessed=1 << 20, transcendentals=0),
            name=name,
        )(*args)

    return run


def local(global_params, local_params, residual, momentum, kept, owner, queries, keys, values):
    islands = lax.axis_size("island")
    shards = lax.axis_size("mp")
    me = lax.axis_index("island").astype(i32).reshape(1)
    rows, columns = global_params.shape
    blocks = owner.shape[0]
    block_rows = rows // blocks
    own_blocks = blocks // islands
    own_rows = own_blocks * block_rows
    owner_row = owner.reshape(1, blocks)
    shape = jax.ShapeDtypeStruct
    outgoing = call(
        functools.partial(pack_kernel, block_rows, own_blocks),
        shape((rows, columns), bf16),
        "pack",
        smem=1,
    )(me, owner_row, kept, global_params, local_params, residual)
    received = lax.all_to_all(
        outgoing.reshape(islands, own_rows, columns), "island", split_axis=0, concat_axis=0, tiled=True
    )
    new_residual, table, mine = call(
        functools.partial(side_kernel, block_rows, own_blocks),
        (
            shape((rows, columns), bf16),
            shape((rows, rows), bf16),
            shape((own_rows, columns), bf16),
        ),
        "side",
        smem=1,
    )(me, owner_row, kept, global_params, local_params, residual)
    attended = attend(queries, keys, values)
    average, squares = call(
        functools.partial(average_kernel, block_rows),
        (shape((own_rows, columns), f32), shape((shards, 128), f32)),
        "average",
    )(received)
    squares = lax.all_to_all(squares, "mp", split_axis=0, concat_axis=0, tiled=True)
    new_moment, fresh = call(
        functools.partial(update_kernel, block_rows, islands),
        (shape((own_rows, columns), f32), shape((islands, own_rows, columns), bf16)),
        "update",
    )(squares, average, momentum, mine)
    everything = lax.all_to_all(fresh, "island", split_axis=0, concat_axis=0, tiled=True)
    merged = call(merge_kernel, shape((rows, columns), bf16), "merge")(table, everything)
    return (merged, new_residual, new_moment, attended)


def solution(mesh):
    placed = (
        P(None, "mp"),
        P("island", "mp"),
        P("island", "mp"),
        P("island", "mp"),
        P(),
        P(),
        P("island", "mp"),
        P("island", "mp"),
        P("island", "mp"),
    )
    return jax.shard_map(
        local,
        mesh=mesh,
        in_specs=placed,
        out_specs=(P(None, "mp"), P("island", "mp"), P("island", "mp"), P("island", "mp")),
        check_vma=False,
    )
```

time: 152 us -> 70.7 us (0.47)
  the two profiles are of different devices: /device:TPU:8 before, /device:TPU:16 now
where the time goes in v1:
time: 70.7 us; the launch traced here: 70.2 us
  blocking collectives  24 us (34%)
  starting transfers between devices  16.1 us (23%)
  waiting for transfers between devices  13 us (18%)
  Pallas kernels  11.6 us (16%)
  local copies, waits for them, and re-layouts  4.83 us (7%)
  between operations  0.76 us (1%)
    all_to_all x1, blocking collectives, local(): lax.all_to_all(outgoing.reshape(islands, own_rows, columns), 'island', sp...  24 us
    all_to_all x1, starting transfers between devices, local(): lax.all_to_all(squares, 'mp', split_axis=0, concat_axis=0, tiled=True)  10.7 us
    all_to_all x1, waiting for transfers between devices, local(): lax.all_to_all(squares, 'mp', split_axis=0, concat_axis=0, tiled=True)  6.87 us
    pallas_call x1, Pallas kernels, attend(): pl.pallas_call(functools.partial(attend_kernel, 256), grid=(heads,), in_s...  6.75 us
    all_to_all x1, waiting for transfers between devices, local(): lax.all_to_all(fresh, 'island', split_axis=0, concat_axis=0, tiled=True)  6.1 us
    all_to_all x1, starting transfers between devices, local(): lax.all_to_all(fresh, 'island', split_axis=0, concat_axis=0, tiled=True)  5.43 us
    pallas_call x5, Pallas kernels, run(): pl.pallas_call(body, in_specs=[pl.BlockSpec(memory_space=pltpu.SMEM)] * s...  4.85 us
    unnamed x24, local copies, waits for them, and re-layouts  4.83 us
  transfers between devices with their start and end apart: 2, of which 2 were waited for; matrix products, arithmetic and copies ran while one was open for 0% of the time, Pallas kernels for 12%

profile of v1, /device:TPU:16, one launch (start us, length us, event | category | flops | bytes accessed | tf_op | source)
XLA Modules:
  0.0 70.2 jit_solution(16752931928813855587)
XLA Ops:
  0.6 0.0 copy-start.7
  0.6 0.0 copy-start.8
  0.7 0.7 copy-done.7
  1.3 0.0 copy-done.8
  1.3 0.0 copy-start
  1.3 1.0 %copy-done = bf16[512,384]{1,0:T(8,128)(2,1)S(1)} copy-done((bf16[512,384]{1,0:T(8,128)(2,1)S(1)}, bf16[512,384]{1,0:T(8,128)(2,1)}, u32[]{:S(2)}) %copy-start) | copy-done | bytes 393240
  2.3 0.0 copy-start.2
  2.3 1.0 %copy-done.2 = bf16[512,384]{1,0:T(8,128)(2,1)S(1)} copy-done((bf16[512,384]{1,0:T(8,128)(2,1)S(1)}, bf16[512,384]{1,0:T(8,128)(2,1)}, u32[]{:S(2)}) %copy-start.2) | copy-done | bytes 393240
  3.3 0.0 copy-start.4
  3.3 1.0 %copy-done.4 = bf16[512,384]{1,0:T(8,128)(2,1)S(1)} copy-done((bf16[512,384]{1,0:T(8,128)(2,1)S(1)}, bf16[512,384]{1,0:T(8,128)(2,1)}, u32[]{:S(2)}) %copy-start.4) | copy-done | bytes 393240
  4.3 0.6 pack.1
  5.0 0.0 copy-start.3
  5.0 0.0 copy-start.5
  5.0 24.0 %all_to_all.21.received_ref = bf16[16,32,384]{2,1,0:T(8,128)(2,1)S(1)} all-to-all(bf16[16,32,384]{2,1,0:T(8,128)(2,1)S(1)} %bitcast.7), channel_id=1, replica_groups=mesh['island'=16,'mp'=32] {'island'}, dimensions={0} | all-to-all | bytes 786432 | tf_op jit(solution)/shard_map/all_to_all | solution.py:215
  28.9 0.0 copy-start.1
  28.9 0.8 %average.1 = (f32[32,384]{1,0:T(8,128)S(1)}, f32[32,128]{1,0:T(8,128)}) custom-call(bf16[16,32,384]{2,1,0:T(8,128)(2,1)S(1)} %all_to_all.21.received_ref), custom_call_target="tpu_custom_call" | custom-call | bytes 1048576 | tf_op jit(solution)/shard_map/average/pallas_call | solution.py:185
  29.7 10.7 %all-to-all-start.1 = ((f32[32,1,128]{2,1,0:T(1,128)}), f32[32,1,128]{2,1,0:T(1,128)S(1)}, u32[]{:S(2)}, u32[]{:S(2)}) async-start(f32[32,1,128]{2,1,0:T(1,128)} %bitcast.4), calls=%async_computation.1 | async-start | bytes 32768 | tf_op jit(solution)/shard_map/all_to_all | solution.py:234
  40.4 0.0 copy-done.3
  40.4 0.0 copy-done.5
  40.4 0.0 copy-done.1
  40.4 0.0 copy-start.6
  40.5 0.0 copy-start.9
  40.5 0.0 copy-start.10
  40.5 1.3 %side.1 = (bf16[512,384]{1,0:T(8,128)(2,1)}, bf16[512,512]{1,0:T(8,128)(2,1)S(1)}, bf16[32,384]{1,0:T(8,128)(2,1)S(1)}) custom-call(s32[1]{0:T(128)} %bitcast.me_ref, s32[1,64]{1,0:T(1,128)S(1)} %bitcast.10, s32[16,16]{1,0:T(8,128)S(1)} %copy-done.7, bf16[512,384]{1,0:T(8,128)(2,1)S(1)} %copy-done.1, bf16[512,384]{1,0:T(8,128)(2,1)S(1)} %copy-done.3, ...), custom_call_target="tpu_custom_call" | custom-call | bytes 1048576 | tf_op jit(solution)/shard_map/side/pallas_call | solution.py:185
  41.8 6.9 %all-to-all-done.1 = f32[32,1,128]{2,1,0:T(1,128)S(1)} async-done(((f32[32,1,128]{2,1,0:T(1,128)}), f32[32,1,128]{2,1,0:T(1,128)S(1)}, u32[]{:S(2)}, u32[]{:S(2)}) %all-to-all-start.1) | async-done | bytes 16416 | tf_op jit(solution)/shard_map/all_to_all | solution.py:234
  48.7 0.0 copy-done.6
  48.7 1.0 %update.1 = (f32[32,384]{1,0:T(8,128)}, bf16[16,32,384]{2,1,0:T(8,128)(2,1)}) custom-call(f32[32,128]{1,0:T(8,128)S(1)} %bitcast.8, f32[32,384]{1,0:T(8,128)S(1)} %get-tuple-element.13.average_ref, f32[32,384]{1,0:T(8,128)S(1)} %copy-done.6, bf16[32,384]{1,0:T(8,128)(2,1)S(1)} %get-tuple-element.14.mine_ref), custom_call_target="tpu_custom_call" | custom-call | bytes 1048576 | tf_op jit(solution)/shard_map/update/pallas_call | solution.py:185
  49.6 5.4 %all-to-all-start.2 = ((bf16[16,32,384]{2,1,0:T(8,128)(2,1)}), bf16[16,32,384]{2,1,0:T(8,128)(2,1)S(1)}, u32[]{:S(2)}, u32[]{:S(2)}) async-start(bf16[16,32,384]{2,1,0:T(8,128)(2,1)} %get-tuple-element.15), calls=%async_computation.2 | async-start | bytes 786432 | tf_op jit(solution)/shard_map/all_to_all | solution.py:240
  55.1 0.0 copy-done.9
  55.1 0.0 copy-done.10
  55.1 0.0 copy-start.11
  55.1 1.1 %copy-done.11 = bf16[1024,384]{1,0:T(8,128)(2,1)S(1)} copy-done((bf16[1024,384]{1,0:T(8,128)(2,1)S(1)}, bf16[1024,384]{1,0:T(8,128)(2,1)}, u32[]{:S(2)}) %copy-start.11) | copy-done | bytes 786456
  56.2 6.8 %attend.1 = bf16[1024,384]{1,0:T(8,128)(2,1)} custom-call(bf16[1024,384]{1,0:T(8,128)(2,1)S(1)} %copy-done.9, bf16[1024,384]{1,0:T(8,128)(2,1)S(1)} %copy-done.10, bf16[1024,384]{1,0:T(8,128)(2,1)S(1)} %copy-done.11), custom_call_target="tpu_custom_call" | custom-call | flops 1207959552 | bytes 3145728 | tf_op jit(solution)/shard_map/attend/pallas_call | solution.py:165
  63.0 6.1 %all-to-all-done.2.fresh_ref = bf16[16,32,384]{2,1,0:T(8,128)(2,1)S(1)} async-done(((bf16[16,32,384]{2,1,0:T(8,128)(2,1)}), bf16[16,32,384]{2,1,0:T(8,128)(2,1)S(1)}, u32[]{:S(2)}, u32[]{:S(2)}) %all-to-all-start.2) | async-done | bytes 393248 | tf_op jit(solution)/shard_map/all_to_all | solution.py:240
  69.1 1.2 %merge.1 = bf16[512,384]{1,0:T(8,128)(2,1)} custom-call(bf16[512,512]{1,0:T(8,128)(2,1)S(1)} %get-tuple-element.11.table_ref, bf16[16,32,384]{2,1,0:T(8,128)(2,1)S(1)} %all-to-all-done.2.fresh_ref), custom_call_target="tpu_custom_call" | custom-call | bytes 1048576 | tf_op jit(solution)/shard_map/merge/pallas_call | solution.py:185
Async XLA Ops:
  0.6 0.7 copy-start.7
  0.6 0.7 copy-start.8
  1.3 1.0 %copy-start = (bf16[512,384]{1,0:T(8,128)(2,1)S(1)}, bf16[512,384]{1,0:T(8,128)(2,1)}, u32[]{:S(2)}) copy-start(bf16[512,384]{1,0:T(8,128)(2,1)} %global_ref.3) | copy-start | bytes 1179652
  2.3 1.0 %copy-start.2 = (bf16[512,384]{1,0:T(8,128)(2,1)S(1)}, bf16[512,384]{1,0:T(8,128)(2,1)}, u32[]{:S(2)}) copy-start(bf16[512,384]{1,0:T(8,128)(2,1)} %local_ref.3) | copy-start | bytes 1179652
  3.3 1.0 %copy-start.4 = (bf16[512,384]{1,0:T(8,128)(2,1)S(1)}, bf16[512,384]{1,0:T(8,128)(2,1)}, u32[]{:S(2)}) copy-start(bf16[512,384]{1,0:T(8,128)(2,1)} %residual_ref.3) | copy-start | bytes 1179652
  5.0 35.4 %copy-start.3 = (bf16[512,384]{1,0:T(8,128)(2,1)S(1)}, bf16[512,384]{1,0:T(8,128)(2,1)}, u32[]{:S(2)}) copy-start(bf16[512,384]{1,0:T(8,128)(2,1)} %local_ref.3) | copy-start | bytes 1179652
  5.0 35.4 %copy-start.5 = (bf16[512,384]{1,0:T(8,128)(2,1)S(1)}, bf16[512,384]{1,0:T(8,128)(2,1)}, u32[]{:S(2)}) copy-start(bf16[512,384]{1,0:T(8,128)(2,1)} %residual_ref.3) | copy-start | bytes 1179652
  28.9 11.5 %copy-start.1 = (bf16[512,384]{1,0:T(8,128)(2,1)S(1)}, bf16[512,384]{1,0:T(8,128)(2,1)}, u32[]{:S(2)}) copy-start(bf16[512,384]{1,0:T(8,128)(2,1)} %global_ref.3) | copy-start | bytes 1179652
  29.7 19.0 %all-to-all-start.1 = ((f32[32,1,128]{2,1,0:T(1,128)}), f32[32,1,128]{2,1,0:T(1,128)S(1)}, u32[]{:S(2)}, u32[]{:S(2)}) async-start(f32[32,1,128]{2,1,0:T(1,128)} %bitcast.4), calls=%async_computation.1 | async-start | bytes 32768 | tf_op jit(solution)/shard_map/all_to_all | solution.py:234
  40.4 8.2 %copy-start.6 = (f32[32,384]{1,0:T(8,128)S(1)}, f32[32,384]{1,0:T(8,128)}, u32[]{:S(2)}) copy-start(f32[32,384]{1,0:T(8,128)} %momentum_ref.1) | copy-start | bytes 147460
  40.5 14.6 %copy-start.9 = (bf16[1024,384]{1,0:T(8,128)(2,1)S(1)}, bf16[1024,384]{1,0:T(8,128)(2,1)}, u32[]{:S(2)}) copy-start(bf16[1024,384]{1,0:T(8,128)(2,1)} %query_ref.1) | copy-start | bytes 2359300
  40.5 14.6 %copy-start.10 = (bf16[1024,384]{1,0:T(8,128)(2,1)S(1)}, bf16[1024,384]{1,0:T(8,128)(2,1)}, u32[]{:S(2)}) copy-start(bf16[1024,384]{1,0:T(8,128)(2,1)} %key_ref.1) | copy-start | bytes 2359300
  49.6 19.4 %all-to-all-start.2 = ((bf16[16,32,384]{2,1,0:T(8,128)(2,1)}), bf16[16,32,384]{2,1,0:T(8,128)(2,1)S(1)}, u32[]{:S(2)}, u32[]{:S(2)}) async-start(bf16[16,32,384]{2,1,0:T(8,128)(2,1)} %get-tuple-element.15), calls=%async_computation.2 | async-start | bytes 786432 | tf_op jit(solution)/shard_map/all_to_all | solution.py:240
  55.1 1.1 %copy-start.11 = (bf16[1024,384]{1,0:T(8,128)(2,1)S(1)}, bf16[1024,384]{1,0:T(8,128)(2,1)}, u32[]{:S(2)}) copy-start(bf16[1024,384]{1,0:T(8,128)(2,1)} %value_ref.1) | copy-start | bytes 2359300

commit v2 on v1

v2 whole, which is shorter than its diff:
```python
import functools
import math

import jax
import jax.numpy as jnp
from jax import lax
from jax.experimental import pallas as pl
from jax.experimental.pallas import tpu as pltpu
from jax.sharding import PartitionSpec as P

D = 12288
HEAD = 128

clip_level = 1.4
momentum_rate = 0.9
outer_rate = 0.7
epsilon = 1e-06

f32 = jnp.float32
bf16 = jnp.bfloat16
i32 = jnp.int32


def iota(shape, axis):
    return lax.broadcasted_iota(i32, shape, axis)


def places(owner_row, kept, me, rows, block_rows, own_blocks):
    blocks = owner_row.shape[1]
    islands = kept.shape[0]
    square = (blocks, blocks)
    sub, lane = iota(square, 0), iota(square, 1)
    owner_col = jnp.sum(jnp.where(sub == lane, owner_row, 0), axis=1, keepdims=True)
    before = (owner_col == owner_row) & (lane < sub)
    slot_col = jnp.sum(before.astype(i32), axis=1, keepdims=True)
    mine = jnp.sum(jnp.where(iota(kept.shape, 0) == me, kept, 0), axis=0, keepdims=True)
    hit = iota((blocks, islands), 1) == owner_col
    limit_col = jnp.sum(jnp.where(hit, mine, 0), axis=1, keepdims=True)
    place_col = (owner_col * own_blocks + slot_col) * block_rows
    wide = (blocks, rows)
    member = iota(wide, 1) // block_rows == iota(wide, 0)
    code_col = jnp.where(slot_col < limit_col, place_col, place_col + rows)
    code = jnp.sum(jnp.where(member, code_col, 0), axis=0, keepdims=True)
    return code + iota((1, rows), 1) % block_rows


def fetch(sources, targets, semaphores):
    copies = []
    for index, (source, target) in enumerate(zip(sources, targets, strict=True)):
        copies.append(pltpu.make_async_copy(source, target, semaphores.at[index]))
        copies[-1].start()
    return copies


def pieces(ref, count):
    step = ref.shape[0] // count
    return [ref.at[pl.ds(part * step, step)] for part in range(count)]


def pack_kernel(
    block_rows, own_blocks, me_ref, owner_hbm, kept_hbm, global_hbm, local_hbm, residual_hbm, out_ref,
    owner_ref, kept_ref, global_ref, local_ref, residual_ref, sem,
):
    rows = global_ref.shape[0]
    copies = fetch(
        (owner_hbm, kept_hbm, global_hbm, local_hbm, residual_hbm),
        (owner_ref, kept_ref, global_ref, local_ref, residual_ref),
        sem,
    )
    for copy in copies[:2]:
        copy.wait()
    code = places(owner_ref[...], kept_ref[...], me_ref[0], rows, block_rows, own_blocks)
    table = jnp.where(iota((rows, rows), 0) == code, 1.0, 0.0).astype(bf16)
    for copy in copies[2:]:
        copy.wait()
    combined = global_ref[...].astype(f32) - local_ref[...].astype(f32) + residual_ref[...].astype(f32)
    out_ref[...] = jnp.dot(table, combined.astype(bf16), preferred_element_type=f32).astype(bf16)


def inner_kernel(
    block_rows, own_blocks, step, me_ref, owner_hbm, kept_hbm, global_hbm, local_hbm, residual_hbm, query_ref, key_ref,
    value_ref, new_hbm, attended_hbm, table_ref, mine_ref, owner_ref, kept_ref, global_ref, local_ref, residual_ref,
    new_ref, attended_ref, in_sem, out_sem,
):
    rows = global_ref.shape[0]
    me = me_ref[0]
    copies = fetch(
        (owner_hbm, kept_hbm, global_hbm, local_hbm, residual_hbm),
        (owner_ref, kept_ref, global_ref, local_ref, residual_ref),
        in_sem,
    )
    tokens, columns = query_ref.shape
    lower = iota((step, step), 0) >= iota((step, step), 1)
    ones = jnp.ones((tokens, HEAD), bf16)
    begins = list(reversed(range(0, tokens, step)))
    stores = []

    def attend_rows(number):
        begin = begins[number]
        for head in range(columns // HEAD):
            attend_block(query_ref, key_ref, value_ref, attended_ref, lower, ones, begin, step, head)
        rng = pl.ds(begin, step)
        stores.extend(fetch((attended_ref.at[rng],), (attended_hbm.at[rng],), out_sem.at[pl.ds(number, 1)]))

    attend_rows(0)
    for copy in copies:
        copy.wait()
    code = places(owner_ref[...], kept_ref[...], me, rows, block_rows, own_blocks)
    code_col = jnp.broadcast_to(code, (8, rows)).astype(f32).T[:, :1].astype(i32)
    fragment = global_ref[...]
    combined = fragment.astype(f32) - local_ref[...].astype(f32) + residual_ref[...].astype(f32)
    kept_part = jnp.where(code_col < rows, combined.astype(bf16).astype(f32), 0.0)
    new_ref[...] = (combined - kept_part).astype(bf16)
    stores.extend(fetch((new_ref,), (new_hbm,), out_sem.at[pl.ds(len(begins), 1)]))
    place_col = jnp.where(code_col < rows, code_col, code_col - rows)
    table_ref[...] = jnp.where(iota((rows, rows), 1) == place_col, 1.0, 0.0).astype(bf16)
    own_rows = own_blocks * block_rows
    place = jnp.where(code < rows, code, code - rows)
    pick = jnp.where(iota((own_rows, rows), 0) + me * own_rows == place, 1.0, 0.0).astype(bf16)
    mine_ref[...] = jnp.dot(pick, fragment, preferred_element_type=f32).astype(bf16)
    for number in range(1, len(begins)):
        attend_rows(number)
    for copy in stores:
        copy.wait()


def attend_block(query_ref, key_ref, value_ref, out_ref, lower, ones, begin, step, head):
    rate = math.log2(math.e) / math.sqrt(HEAD)
    across = (((1,), (1,)), ((), ()))
    cols = slice(head * HEAD, (head + 1) * HEAD)
    end = begin + step
    query = query_ref[begin:end, cols]
    corner = lax.dot_general(query, key_ref[begin:end, cols], across, preferred_element_type=f32)
    corner = jnp.where(lower, corner, -jnp.inf)
    top = jnp.max(corner, axis=1, keepdims=True)
    if begin:
        past = lax.dot_general(query, key_ref[:begin, cols], across, preferred_element_type=f32)
        top = jnp.maximum(top, jnp.max(past, axis=1, keepdims=True))
    expo = jnp.exp2((corner - top) * rate).astype(bf16)
    mixed = jnp.dot(expo, jnp.concatenate([value_ref[begin:end, cols], ones[begin:end]], axis=1), preferred_element_type=f32)
    if begin:
        expo = jnp.exp2((past - top) * rate).astype(bf16)
        mixed = mixed + jnp.dot(
            expo, jnp.concatenate([value_ref[:begin, cols], ones[:begin]], axis=1), preferred_element_type=f32
        )
    out_ref[begin:end, cols] = (mixed[:, :HEAD] / mixed[:, HEAD : HEAD + 1]).astype(bf16)


def average_kernel(block_rows, received_ref, average_ref, square_ref):
    islands, own_rows, _ = received_ref.shape
    average = jnp.sum(received_ref[...].astype(f32), axis=0) / islands
    average_ref[...] = average
    squares = average * average
    lane = iota((1, 128), 1)
    row = jnp.zeros((1, 128), f32)
    for block in range(own_rows // block_rows):
        part = squares[block * block_rows : (block + 1) * block_rows]
        total = jnp.sum(jnp.sum(part, axis=0, keepdims=True), axis=1, keepdims=True)
        row = jnp.where(lane == block, total, row)
    square_ref[...] = jnp.broadcast_to(row, square_ref.shape)


def block_factors(square_ref, block_rows, own_rows, islands):
    total = jnp.sum(square_ref[...], axis=0, keepdims=True)
    root = jnp.sqrt(total / (block_rows * D) + epsilon)
    factor = jnp.minimum(1.0, clip_level / math.sqrt(islands) / root)
    shape = (own_rows, factor.shape[1])
    hit = iota(shape, 0) // block_rows == iota(shape, 1)
    return jnp.sum(jnp.where(hit, factor, 0.0), axis=1, keepdims=True)


def update_kernel(block_rows, square_ref, average_ref, momentum_ref, mine_ref, fresh_ref):
    islands, own_rows, _ = fresh_ref.shape
    clipped = average_ref[...] * block_factors(square_ref, block_rows, own_rows, islands)
    moment = momentum_rate * momentum_ref[...] + clipped
    update = clipped + momentum_rate * moment
    fresh = (mine_ref[...].astype(f32) - outer_rate * update).astype(bf16)
    for island in range(islands):
        fresh_ref[island] = fresh


def merge_kernel(
    block_rows, parts, square_ref, average_ref, momentum_ref, table_ref, fresh_ref, moment_hbm, out_hbm,
    moment_ref, out_ref, out_sem,
):
    islands, own_rows, columns = fresh_ref.shape
    clipped = average_ref[...] * block_factors(square_ref, block_rows, own_rows, islands)
    moment_ref[...] = momentum_rate * momentum_ref[...] + clipped
    stores = fetch((moment_ref,), (moment_hbm,), out_sem.at[pl.ds(parts, 1)])
    step = islands * own_rows // parts
    fresh = fresh_ref[...].reshape(islands * own_rows, columns)
    for part in range(parts):
        rng = slice(part * step, (part + 1) * step)
        out_ref[rng, :] = jnp.dot(table_ref[rng, :], fresh, preferred_element_type=f32).astype(bf16)
        rng = pl.ds(part * step, step)
        stores += fetch((out_ref.at[rng],), (out_hbm.at[rng],), out_sem.at[pl.ds(part, 1)])
    for copy in stores:
        copy.wait()


def call(body, name, in_spaces, out_spaces, out_shape, scratch=(), flops=0):
    def run(*args):
        args = [
            pltpu.with_memory_space_constraint(arg, space) if space == pltpu.HBM else arg
            for arg, space in zip(args, in_spaces, strict=True)
        ]
        return pl.pallas_call(
            body,
            in_specs=[pl.BlockSpec(memory_space=space) for space in in_spaces],
            out_specs=jax.tree.map(lambda space: pl.BlockSpec(memory_space=space), out_spaces),
            out_shape=out_shape,
            scratch_shapes=scratch,
            compiler_params=pltpu.CompilerParams(vmem_limit_bytes=32 << 20),
            cost_estimate=pl.CostEstimate(flops=flops, bytes_accessed=1 << 20, transcendentals=0),
            name=name,
        )(*args)

    return run


def local(global_params, local_params, residual, momentum, kept, owner, queries, keys, values):
    islands = lax.axis_size("island")
    shards = lax.axis_size("mp")
    me = lax.axis_index("island").astype(i32).reshape(1)
    rows, columns = global_params.shape
    tokens = queries.shape[0]
    blocks = owner.shape[0]
    block_rows = rows // blocks
    own_blocks = blocks // islands
    own_rows = own_blocks * block_rows
    owner_row = owner.reshape(1, blocks)
    shape = jax.ShapeDtypeStruct
    dma = pltpu.SemaphoreType.DMA
    vmem, smem, hbm = pltpu.VMEM, pltpu.SMEM, pltpu.HBM
    staged = [
        vmem((1, blocks), i32),
        vmem((islands, islands), i32),
        vmem((rows, columns), bf16),
        vmem((rows, columns), bf16),
        vmem((rows, columns), bf16),
    ]
    outgoing = call(
        functools.partial(pack_kernel, block_rows, own_blocks),
        "pack",
        [smem] + [hbm] * 5,
        vmem,
        shape((rows, columns), bf16),
        staged + [dma((5,))],
    )(me, owner_row, kept, global_params, local_params, residual)
    received = lax.all_to_all(
        outgoing.reshape(islands, own_rows, columns), "island", split_axis=0, concat_axis=0, tiled=True
    )
    average, squares = call(
        functools.partial(average_kernel, block_rows),
        "average",
        [vmem],
        (vmem, vmem),
        (shape((own_rows, columns), f32), shape((shards, 128), f32)),
    )(received)
    me, squares = lax.optimization_barrier((me, squares))
    squares = lax.all_to_all(squares, "mp", split_axis=0, concat_axis=0, tiled=True)
    step = min(256, tokens)
    new_residual, attended, table, mine = call(
        functools.partial(inner_kernel, block_rows, own_blocks, step),
        "inner",
        [smem] + [hbm] * 5 + [vmem] * 3,
        (hbm, hbm, vmem, vmem),
        (
            shape((rows, columns), bf16),
            shape((tokens, columns), bf16),
            shape((rows, rows), bf16),
            shape((own_rows, columns), bf16),
        ),
        staged + [vmem((rows, columns), bf16), vmem((tokens, columns), bf16), dma((5,)), dma((1 + tokens // step,))],
        flops=3 * tokens * tokens * columns,
    )(me, owner_row, kept, global_params, local_params, residual, queries, keys, values)
    fresh = call(
        functools.partial(update_kernel, block_rows),
        "update",
        [vmem] * 4,
        vmem,
        shape((islands, own_rows, columns), bf16),
    )(squares, average, momentum, mine)
    everything = lax.all_to_all(fresh, "island", split_axis=0, concat_axis=0, tiled=True)
    parts = 4
    new_moment, merged = call(
        functools.partial(merge_kernel, block_rows, parts),
        "merge",
        [vmem] * 5,
        (hbm, hbm),
        (shape((own_rows, columns), f32), shape((rows, columns), bf16)),
        [vmem((own_rows, columns), f32), vmem((rows, columns), bf16), dma((parts + 1,))],
    )(squares, average, momentum, table, everything)
    return (merged, new_residual, new_moment, attended)


def solution(mesh):
    placed = (
        P(None, "mp"),
        P("island", "mp"),
        P("island", "mp"),
        P("island", "mp"),
        P(),
        P(),
        P("island", "mp"),
        P("island", "mp"),
        P("island", "mp"),
    )
    return jax.shard_map(
        local,
        mesh=mesh,
        in_specs=placed,
        out_specs=(P(None, "mp"), P("island", "mp"), P("island", "mp"), P("island", "mp")),
        check_vma=False,
    )
```

time: 70.7 us -> 67 us (0.948)
  blocking collectives: 24 us -> 43.2 us
  waiting for transfers between devices: 13 us -> 3.2 us
  starting transfers between devices: 16.1 us -> 10.7 us
  local copies, waits for them, and re-layouts: 4.83 us -> 0.02 us
  Pallas kernels: 11.6 us -> 8.93 us
    all_to_all x0 -> x1, blocking collectives: none -> 19.2 us  [local(): lax.all_to_all(fresh, 'island', split_axis=0, concat_axis=0, tiled=True)]
    all_to_all x1 -> x0, waiting for transfers between devices: 6.1 us -> none  [local(): lax.all_to_all(fresh, 'island', split_axis=0, concat_axis=0, tiled=True)]
    all_to_all x1 -> x0, starting transfers between devices: 5.43 us -> none  [local(): lax.all_to_all(fresh, 'island', split_axis=0, concat_axis=0, tiled=True)]
    unnamed x24 -> x8, local copies, waits for them, and re-layouts: 4.83 us -> 0.02 us
    all_to_all x1, waiting for transfers between devices: 6.87 us -> 3.2 us  [local(): lax.all_to_all(squares, 'mp', split_axis=0, concat_axis=0, tiled=True)]
    pallas_call x6 -> x5, Pallas kernels: 11.6 us -> 8.93 us  [run(): pl.pallas_call(body, in_specs=[pl.BlockSpec(memory_space=space) for space...]
  transfers between devices with their start and end apart: 2 -> 1, of which waited for: 2 -> 1; matrix products, arithmetic and copies ran while one was open for 0% -> 0% of each run, Pallas kernels for 12% -> 7%
where the time goes in v2:
time: 67 us; the launch traced here: 66.8 us
  blocking collectives  43.2 us (64%)
  starting transfers between devices  10.7 us (16%)
  Pallas kernels  8.93 us (13%)
  waiting for transfers between devices  3.2 us (5%)
  between operations  0.72 us (1%)
    all_to_all x1, blocking collectives, local(): lax.all_to_all(outgoing.reshape(islands, own_rows, columns), 'island', sp...  24 us
    all_to_all x1, blocking collectives, local(): lax.all_to_all(fresh, 'island', split_axis=0, concat_axis=0, tiled=True)  19.2 us
    all_to_all x1, starting transfers between devices, local(): lax.all_to_all(squares, 'mp', split_axis=0, concat_axis=0, tiled=True)  10.7 us
    pallas_call x5, Pallas kernels, run(): pl.pallas_call(body, in_specs=[pl.BlockSpec(memory_space=space) for space...  8.93 us
    all_to_all x1, waiting for transfers between devices, local(): lax.all_to_all(squares, 'mp', split_axis=0, concat_axis=0, tiled=True)  3.2 us
  transfers between devices with their start and end apart: 1, of which 1 were waited for; matrix products, arithmetic and copies ran while one was open for 0% of the time, Pallas kernels for 7%

profile of v2, /device:TPU:16, one launch (start us, length us, event | category | flops | bytes accessed | tf_op | source)
XLA Modules:
  0.0 66.8 jit_solution(9712302646844108664)
XLA Ops:
  0.6 0.0 copy-start.2
  0.6 0.0 copy-start.3
  0.7 1.9 %pack.1 = bf16[512,384]{1,0:T(8,128)(2,1)S(1)} custom-call(s32[1]{0:T(128)} %bitcast.me_ref, s32[1,64]{1,0:T(1,128)} %bitcast.10, s32[16,16]{1,0:T(8,128)} %kept_hbm.3, bf16[512,384]{1,0:T(8,128)(2,1)} %global_hbm.3, bf16[512,384]{1,0:T(8,128)(2,1)} %local_hbm.3, bf16[512,384]{1,0:T(8,128)(2,1)} %residual_hbm.3), custom_call_target="tpu_custom_call" | custom-call | bytes 1048576 | tf_op jit(solution)/shard_map/pack/pallas_call | solution.py:207
  2.6 0.0 copy-start.1
  2.6 24.0 %all_to_all.21.received_ref = bf16[16,32,384]{2,1,0:T(8,128)(2,1)S(1)} all-to-all(bf16[16,32,384]{2,1,0:T(8,128)(2,1)S(1)} %bitcast.7), channel_id=1, replica_groups=mesh['island'=16,'mp'=32] {'island'}, dimensions={0} | all-to-all | bytes 786432 | tf_op jit(solution)/shard_map/all_to_all | solution.py:250
  26.5 0.8 %average.1 = (f32[32,384]{1,0:T(8,128)S(1)}, f32[32,128]{1,0:T(8,128)}) custom-call(bf16[16,32,384]{2,1,0:T(8,128)(2,1)S(1)} %all_to_all.21.received_ref), custom_call_target="tpu_custom_call" | custom-call | bytes 1048576 | tf_op jit(solution)/shard_map/average/pallas_call | solution.py:207
  27.3 10.7 %all-to-all-start.1 = ((f32[32,1,128]{2,1,0:T(1,128)}), f32[32,1,128]{2,1,0:T(1,128)S(1)}, u32[]{:S(2)}, u32[]{:S(2)}) async-start(f32[32,1,128]{2,1,0:T(1,128)} %bitcast.4), calls=%async_computation.1 | async-start | bytes 32768 | tf_op jit(solution)/shard_map/all_to_all | solution.py:261
  38.0 0.0 copy-done.2
  38.0 0.0 copy-done.3
  38.0 0.0 copy-done.1
  38.0 0.0 copy-start
  38.1 5.0 %inner.1 = (bf16[512,384]{1,0:T(8,128)(2,1)}, bf16[1024,384]{1,0:T(8,128)(2,1)}, bf16[512,512]{1,0:T(8,128)(2,1)S(1)}, bf16[32,384]{1,0:T(8,128)(2,1)S(1)}) custom-call(s32[1]{0:T(128)} %bitcast.me_ref, s32[1,64]{1,0:T(1,128)} %bitcast.11, s32[16,16]{1,0:T(8,128)} %kept_hbm.3, bf16[512,384]{1,0:T(8,128)(2,1)} %global_hbm.3, bf16[512,384]{1,0:T(8,128)(2,1)} %local_hbm.3, ...), custom_call_target="tpu_custom_call" | custom-call | flops 1207959552 | bytes 1048576 | tf_op jit(solution)/shard_map/inner/pallas_call | solution.py:207
  43.1 3.2 %all-to-all-done.1 = f32[32,1,128]{2,1,0:T(1,128)S(1)} async-done(((f32[32,1,128]{2,1,0:T(1,128)}), f32[32,1,128]{2,1,0:T(1,128)S(1)}, u32[]{:S(2)}, u32[]{:S(2)}) %all-to-all-start.1) | async-done | bytes 16416 | tf_op jit(solution)/shard_map/all_to_all | solution.py:261
  46.3 0.0 copy-done
  46.3 0.1 update.1
  46.4 19.2 %all_to_all.22.fresh_ref = bf16[16,32,384]{2,1,0:T(8,128)(2,1)S(1)} all-to-all(bf16[16,32,384]{2,1,0:T(8,128)(2,1)S(1)} %update.1), channel_id=1, replica_groups=mesh['island'=16,'mp'=32] {'island'}, dimensions={0} | all-to-all | bytes 786432 | tf_op jit(solution)/shard_map/all_to_all | solution.py:284
  65.7 1.1 %merge.1 = (f32[32,384]{1,0:T(8,128)}, bf16[512,384]{1,0:T(8,128)(2,1)}) custom-call(f32[32,128]{1,0:T(8,128)S(1)} %bitcast.9, f32[32,384]{1,0:T(8,128)S(1)} %get-tuple-element.16.average_ref, f32[32,384]{1,0:T(8,128)S(1)} %copy-done, bf16[512,512]{1,0:T(8,128)(2,1)S(1)} %get-tuple-element.18.table_ref, bf16[16,32,384]{2,1,0:T(8,128)(2,1)S(1)} %all_to_all.22.fresh_ref), custom_call_target="tpu_custom_call" | custom-call | bytes 1048576 | tf_op jit(solution)/shard_map/merge/pallas_call | solution.py:207
Async XLA Ops:
  0.6 37.4 %copy-start.2 = (bf16[1024,384]{1,0:T(8,128)(2,1)S(1)}, bf16[1024,384]{1,0:T(8,128)(2,1)}, u32[]{:S(2)}) copy-start(bf16[1024,384]{1,0:T(8,128)(2,1)} %key_ref.1) | copy-start | bytes 2359300
  0.6 37.4 %copy-start.3 = (bf16[1024,384]{1,0:T(8,128)(2,1)S(1)}, bf16[1024,384]{1,0:T(8,128)(2,1)}, u32[]{:S(2)}) copy-start(bf16[1024,384]{1,0:T(8,128)(2,1)} %value_ref.1) | copy-start | bytes 2359300
  2.6 35.5 %copy-start.1 = (bf16[1024,384]{1,0:T(8,128)(2,1)S(1)}, bf16[1024,384]{1,0:T(8,128)(2,1)}, u32[]{:S(2)}) copy-start(bf16[1024,384]{1,0:T(8,128)(2,1)} %query_ref.1) | copy-start | bytes 2359300
  27.3 19.0 %all-to-all-start.1 = ((f32[32,1,128]{2,1,0:T(1,128)}), f32[32,1,128]{2,1,0:T(1,128)S(1)}, u32[]{:S(2)}, u32[]{:S(2)}) async-start(f32[32,1,128]{2,1,0:T(1,128)} %bitcast.4), calls=%async_computation.1 | async-start | bytes 32768 | tf_op jit(solution)/shard_map/all_to_all | solution.py:261
  38.0 8.2 %copy-start = (f32[32,384]{1,0:T(8,128)S(1)}, f32[32,384]{1,0:T(8,128)}, u32[]{:S(2)}) copy-start(f32[32,384]{1,0:T(8,128)} %momentum_ref.3) | copy-start | bytes 147460

commit v3 on v2

--- a/solution.py
+++ b/solution.py
@@ -58,7 +58,7 @@
 
 
 def pack_kernel(
-    block_rows, own_blocks, me_ref, owner_hbm, kept_hbm, global_hbm, local_hbm, residual_hbm, out_ref,
+    block_rows, own_blocks, me_ref, owner_hbm, kept_hbm, global_hbm, local_hbm, residual_hbm, out_ref, code_ref,
     owner_ref, kept_ref, global_ref, local_ref, residual_ref, sem,
 ):
     rows = global_ref.shape[0]
@@ -70,6 +70,7 @@
     for copy in copies[:2]:
         copy.wait()
     code = places(owner_ref[...], kept_ref[...], me_ref[0], rows, block_rows, own_blocks)
+    code_ref[...] = jnp.broadcast_to(code, code_ref.shape)
     table = jnp.where(iota((rows, rows), 0) == code, 1.0, 0.0).astype(bf16)
     for copy in copies[2:]:
         copy.wait()
@@ -77,18 +78,16 @@
     out_ref[...] = jnp.dot(table, combined.astype(bf16), preferred_element_type=f32).astype(bf16)
 
 
+def as_column(code_ref):
+    return code_ref[...].astype(f32).T[:, :1].astype(i32)
+
+
 def inner_kernel(
-    block_rows, own_blocks, step, me_ref, owner_hbm, kept_hbm, global_hbm, local_hbm, residual_hbm, query_ref, key_ref,
-    value_ref, new_hbm, attended_hbm, table_ref, mine_ref, owner_ref, kept_ref, global_ref, local_ref, residual_ref,
-    new_ref, attended_ref, in_sem, out_sem,
+    step, code_ref, global_hbm, local_hbm, residual_hbm, query_ref, key_ref, value_ref, new_hbm, attended_hbm,
+    global_ref, local_ref, residual_ref, new_ref, attended_ref, in_sem, out_sem,
 ):
     rows = global_ref.shape[0]
-    me = me_ref[0]
-    copies = fetch(
-        (owner_hbm, kept_hbm, global_hbm, local_hbm, residual_hbm),
-        (owner_ref, kept_ref, global_ref, local_ref, residual_ref),
-        in_sem,
-    )
+    copies = fetch((global_hbm, local_hbm, residual_hbm), (global_ref, local_ref, residual_ref), in_sem)
     tokens, columns = query_ref.shape
     lower = iota((step, step), 0) >= iota((step, step), 1)
     ones = jnp.ones((tokens, HEAD), bf16)
@@ -105,19 +104,10 @@
     attend_rows(0)
     for copy in copies:
         copy.wait()
-    code = places(owner_ref[...], kept_ref[...], me, rows, block_rows, own_blocks)
-    code_col = jnp.broadcast_to(code, (8, rows)).astype(f32).T[:, :1].astype(i32)
-    fragment = global_ref[...]
-    combined = fragment.astype(f32) - local_ref[...].astype(f32) + residual_ref[...].astype(f32)
-    kept_part = jnp.where(code_col < rows, combined.astype(bf16).astype(f32), 0.0)
+    combined = global_ref[...].astype(f32) - local_ref[...].astype(f32) + residual_ref[...].astype(f32)
+    kept_part = jnp.where(as_column(code_ref) < rows, combined.astype(bf16).astype(f32), 0.0)
     new_ref[...] = (combined - kept_part).astype(bf16)
     stores.extend(fetch((new_ref,), (new_hbm,), out_sem.at[pl.ds(len(begins), 1)]))
-    place_col = jnp.where(code_col < rows, code_col, code_col - rows)
-    table_ref[...] = jnp.where(iota((rows, rows), 1) == place_col, 1.0, 0.0).astype(bf16)
-    own_rows = own_blocks * block_rows
-    place = jnp.where(code < rows, code, code - rows)
-    pick = jnp.where(iota((own_rows, rows), 0) + me * own_rows == place, 1.0, 0.0).astype(bf16)
-    mine_ref[...] = jnp.dot(pick, fragment, preferred_element_type=f32).astype(bf16)
     for number in range(1, len(begins)):
         attend_rows(number)
     for copy in stores:
@@ -146,7 +136,9 @@
     out_ref[begin:end, cols] = (mixed[:, :HEAD] / mixed[:, HEAD : HEAD + 1]).astype(bf16)
 
 
-def average_kernel(block_rows, received_ref, average_ref, square_ref):
+def average_kernel(
+    block_rows, me_ref, received_ref, code_ref, global_ref, average_ref, square_hbm, table_ref, mine_ref, square_ref, sem
+):
     islands, own_rows, _ = received_ref.shape
     average = jnp.sum(received_ref[...].astype(f32), axis=0) / islands
     average_ref[...] = average
@@ -158,6 +150,17 @@
         total = jnp.sum(jnp.sum(part, axis=0, keepdims=True), axis=1, keepdims=True)
         row = jnp.where(lane == block, total, row)
     square_ref[...] = jnp.broadcast_to(row, square_ref.shape)
+    stores = fetch((square_ref,), (square_hbm,), sem)
+    rows = global_ref.shape[0]
+    code = code_ref[0:1, :]
+    place = jnp.where(code < rows, code, code - rows)
+    pick = jnp.where(iota((own_rows, rows), 0) + me_ref[0] * own_rows == place, 1.0, 0.0).astype(bf16)
+    mine_ref[...] = jnp.dot(pick, global_ref[...], preferred_element_type=f32).astype(bf16)
+    code_col = as_column(code_ref)
+    place_col = jnp.where(code_col < rows, code_col, code_col - rows)
+    table_ref[...] = jnp.where(iota((rows, rows), 1) == place_col, 1.0, 0.0).astype(bf16)
+    for copy in stores:
+        copy.wait()
 
 
 def block_factors(square_ref, block_rows, own_rows, islands):
@@ -239,41 +242,47 @@
         vmem((rows, columns), bf16),
         vmem((rows, columns), bf16),
     ]
-    outgoing = call(
+    outgoing, code = call(
         functools.partial(pack_kernel, block_rows, own_blocks),
         "pack",
         [smem] + [hbm] * 5,
-        vmem,
-        shape((rows, columns), bf16),
+        (vmem, vmem),
+        (shape((rows, columns), bf16), shape((8, rows), i32)),
         staged + [dma((5,))],
     )(me, owner_row, kept, global_params, local_params, residual)
+    outgoing, queries, keys, values, momentum = lax.optimization_barrier(
+        (outgoing, queries, keys, values, momentum)
+    )
     received = lax.all_to_all(
         outgoing.reshape(islands, own_rows, columns), "island", split_axis=0, concat_axis=0, tiled=True
     )
-    average, squares = call(
+    average, squares, table, mine = call(
         functools.partial(average_kernel, block_rows),
         "average",
-        [vmem],
-        (vmem, vmem),
-        (shape((own_rows, columns), f32), shape((shards, 128), f32)),
-    )(received)
-    me, squares = lax.optimization_barrier((me, squares))
-    squares = lax.all_to_all(squares, "mp", split_axis=0, concat_axis=0, tiled=True)
-    step = min(256, tokens)
-    new_residual, attended, table, mine = call(
-        functools.partial(inner_kernel, block_rows, own_blocks, step),
-        "inner",
-        [smem] + [hbm] * 5 + [vmem] * 3,
-        (hbm, hbm, vmem, vmem),
+        [smem] + [vmem] * 3,
+        (vmem, hbm, vmem, vmem),
         (
-            shape((rows, columns), bf16),
-            shape((tokens, columns), bf16),
+            shape((own_rows, columns), f32),
+            shape((shards, 128), f32),
             shape((rows, rows), bf16),
             shape((own_rows, columns), bf16),
         ),
-        staged + [vmem((rows, columns), bf16), vmem((tokens, columns), bf16), dma((5,)), dma((1 + tokens // step,))],
+        [vmem((shards, 128), f32), dma((1,))],
+    )(me, received, code, global_params)
+    code, squares = lax.optimization_barrier((code, squares))
+    squares = lax.all_to_all(squares, "mp", split_axis=0, concat_axis=0, tiled=True)
+    step = min(256, tokens)
+    new_residual, attended = call(
+        functools.partial(inner_kernel, step),
+        "inner",
+        [vmem] + [hbm] * 3 + [vmem] * 3,
+        (hbm, hbm),
+        (shape((rows, columns), bf16), shape((tokens, columns), bf16)),
+        staged[2:]
+        + [vmem((rows, columns), bf16), vmem((tokens, columns), bf16), dma((3,)), dma((1 + tokens // step,))],
         flops=3 * tokens * tokens * columns,
-    )(me, owner_row, kept, global_params, local_params, residual, queries, keys, values)
+    )(code, global_params, local_params, residual, queries, keys, values)
+    mine, new_residual = lax.optimization_barrier((mine, new_residual))
     fresh = call(
         functools.partial(update_kernel, block_rows),
         "update",

time: 67 us -> 67.1 us (level)
  no operation moved by 1% of the time
where the time goes in v3:
time: 67.1 us; the launch traced here: 66.9 us
  blocking collectives  43.2 us (64%)
  starting transfers between devices  10.7 us (16%)
  Pallas kernels  8.68 us (13%)
  waiting for transfers between devices  3.54 us (5%)
  between operations  0.74 us (1%)
    all_to_all x1, blocking collectives, local(): lax.all_to_all(outgoing.reshape(islands, own_rows, columns), 'island', sp...  24 us
    all_to_all x1, blocking collectives, local(): lax.all_to_all(fresh, 'island', split_axis=0, concat_axis=0, tiled=True)  19.2 us
    all_to_all x1, starting transfers between devices, local(): lax.all_to_all(squares, 'mp', split_axis=0, concat_axis=0, tiled=True)  10.7 us
    pallas_call x5, Pallas kernels, run(): pl.pallas_call(body, in_specs=[pl.BlockSpec(memory_space=space) for space...  8.68 us
    all_to_all x1, waiting for transfers between devices, local(): lax.all_to_all(squares, 'mp', split_axis=0, concat_axis=0, tiled=True)  3.54 us
  transfers between devices with their start and end apart: 1, of which 1 were waited for; matrix products, arithmetic and copies ran while one was open for 0% of the time, Pallas kernels for 7%

profile of v3, /device:TPU:16, one launch (start us, length us, event | category | flops | bytes accessed | tf_op | source)
XLA Modules:
  0.0 66.9 jit_solution(9727074195425564709)
XLA Ops:
  0.6 0.0 copy-start.3
  0.6 0.0 copy-start.4
  0.7 1.9 %pack.1 = (bf16[512,384]{1,0:T(8,128)(2,1)S(1)}, s32[8,512]{1,0:T(8,128)S(1)}) custom-call(s32[1]{0:T(128)} %bitcast.me_ref, s32[1,64]{1,0:T(1,128)} %bitcast.10, s32[16,16]{1,0:T(8,128)} %kept_hbm.1, bf16[512,384]{1,0:T(8,128)(2,1)} %global_hbm.3, bf16[512,384]{1,0:T(8,128)(2,1)} %local_hbm.3, bf16[512,384]{1,0:T(8,128)(2,1)} %residual_hbm.3), custom_call_target="tpu_custom_call" | custom-call | bytes 1048576 | tf_op jit(solution)/shard_map/pack/pallas_call | solution.py:210
  2.6 0.0 copy-start
  2.6 0.0 copy-start.2
  2.6 24.0 %all_to_all.21.received_ref = bf16[16,32,384]{2,1,0:T(8,128)(2,1)S(1)} all-to-all(bf16[16,32,384]{2,1,0:T(8,128)(2,1)S(1)} %bitcast.7), channel_id=1, replica_groups=mesh['island'=16,'mp'=32] {'island'}, dimensions={0} | all-to-all | bytes 786432 | tf_op jit(solution)/shard_map/all_to_all | solution.py:256
  26.6 0.0 copy-done
  26.6 0.8 %average.1 = (f32[32,384]{1,0:T(8,128)S(1)}, f32[32,128]{1,0:T(8,128)}, bf16[512,512]{1,0:T(8,128)(2,1)S(1)}, bf16[32,384]{1,0:T(8,128)(2,1)S(1)}) custom-call(s32[1]{0:T(128)} %bitcast.me_ref, bf16[16,32,384]{2,1,0:T(8,128)(2,1)S(1)} %all_to_all.21.received_ref, s32[8,512]{1,0:T(8,128)S(1)} %get-tuple-element.32.code_ref, bf16[512,384]{1,0:T(8,128)(2,1)S(1)} %copy-done), custom_call_target="tpu_custom_call" | custom-call | bytes 1048576 | tf_op jit(solution)/shard_map/average/pallas_call | solution.py:210
  27.4 10.7 %all-to-all-start.1 = ((f32[32,1,128]{2,1,0:T(1,128)}), f32[32,1,128]{2,1,0:T(1,128)S(1)}, u32[]{:S(2)}, u32[]{:S(2)}) async-start(f32[32,1,128]{2,1,0:T(1,128)} %bitcast.4), calls=%async_computation.1 | async-start | bytes 32768 | tf_op jit(solution)/shard_map/all_to_all | solution.py:273
  38.1 0.0 copy-done.3
  38.1 0.0 copy-done.4
  38.2 0.0 copy-done.2
  38.2 0.0 copy-start.1
  38.2 4.7 %inner.1 = (bf16[512,384]{1,0:T(8,128)(2,1)}, bf16[1024,384]{1,0:T(8,128)(2,1)}) custom-call(s32[8,512]{1,0:T(8,128)S(1)} %get-tuple-element.32.code_ref, bf16[512,384]{1,0:T(8,128)(2,1)} %global_hbm.3, bf16[512,384]{1,0:T(8,128)(2,1)} %local_hbm.3, bf16[512,384]{1,0:T(8,128)(2,1)} %residual_hbm.3, bf16[1024,384]{1,0:T(8,128)(2,1)S(1)} %copy-done.2, ...), custom_call_target="tpu_custom_call" | custom-call | flops 1207959552 | bytes 1048576 | tf_op jit(solution)/shard_map/inner/pallas_call | solution.py:210
  42.9 3.5 %all-to-all-done.1 = f32[32,1,128]{2,1,0:T(1,128)S(1)} async-done(((f32[32,1,128]{2,1,0:T(1,128)}), f32[32,1,128]{2,1,0:T(1,128)S(1)}, u32[]{:S(2)}, u32[]{:S(2)}) %all-to-all-start.1) | async-done | bytes 16416 | tf_op jit(solution)/shard_map/all_to_all | solution.py:273
  46.4 0.0 copy-done.1
  46.4 0.1 update.1
  46.5 19.2 %all_to_all.22.fresh_ref = bf16[16,32,384]{2,1,0:T(8,128)(2,1)S(1)} all-to-all(bf16[16,32,384]{2,1,0:T(8,128)(2,1)S(1)} %update.1), channel_id=1, replica_groups=mesh['island'=16,'mp'=32] {'island'}, dimensions={0} | all-to-all | bytes 786432 | tf_op jit(solution)/shard_map/all_to_all | solution.py:293
  65.8 1.1 %merge.1 = (f32[32,384]{1,0:T(8,128)}, bf16[512,384]{1,0:T(8,128)(2,1)}) custom-call(f32[32,128]{1,0:T(8,128)S(1)} %bitcast.9, f32[32,384]{1,0:T(8,128)S(1)} %get-tuple-element.28.average_ref, f32[32,384]{1,0:T(8,128)S(1)} %copy-done.1, bf16[512,512]{1,0:T(8,128)(2,1)S(1)} %get-tuple-element.30.table_ref, bf16[16,32,384]{2,1,0:T(8,128)(2,1)S(1)} %all_to_all.22.fresh_ref), custom_call_target="tpu_custom_call" | custom-call | bytes 1048576 | tf_op jit(solution)/shard_map/merge/pallas_call | solution.py:210
Async XLA Ops:
  0.6 37.5 %copy-start.3 = (bf16[1024,384]{1,0:T(8,128)(2,1)S(1)}, bf16[1024,384]{1,0:T(8,128)(2,1)}, u32[]{:S(2)}) copy-start(bf16[1024,384]{1,0:T(8,128)(2,1)} %key_ref) | copy-start | bytes 2359300
  0.6 37.5 %copy-start.4 = (bf16[1024,384]{1,0:T(8,128)(2,1)S(1)}, bf16[1024,384]{1,0:T(8,128)(2,1)}, u32[]{:S(2)}) copy-start(bf16[1024,384]{1,0:T(8,128)(2,1)} %value_ref) | copy-start | bytes 2359300
  2.6 24.0 %copy-start = (bf16[512,384]{1,0:T(8,128)(2,1)S(1)}, bf16[512,384]{1,0:T(8,128)(2,1)}, u32[]{:S(2)}) copy-start(bf16[512,384]{1,0:T(8,128)(2,1)} %global_hbm.3) | copy-start | bytes 1179652
  2.6 35.6 %copy-start.2 = (bf16[1024,384]{1,0:T(8,128)(2,1)S(1)}, bf16[1024,384]{1,0:T(8,128)(2,1)}, u32[]{:S(2)}) copy-start(bf16[1024,384]{1,0:T(8,128)(2,1)} %query_ref) | copy-start | bytes 2359300
  27.4 19.0 %all-to-all-start.1 = ((f32[32,1,128]{2,1,0:T(1,128)}), f32[32,1,128]{2,1,0:T(1,128)S(1)}, u32[]{:S(2)}, u32[]{:S(2)}) async-start(f32[32,1,128]{2,1,0:T(1,128)} %bitcast.4), calls=%async_computation.1 | async-start | bytes 32768 | tf_op jit(solution)/shard_map/all_to_all | solution.py:273
  38.2 8.2 %copy-start.1 = (f32[32,384]{1,0:T(8,128)S(1)}, f32[32,384]{1,0:T(8,128)}, u32[]{:S(2)}) copy-start(f32[32,384]{1,0:T(8,128)} %momentum_ref.1) | copy-start | bytes 147460

commit v4 on v2

--- a/solution.py
+++ b/solution.py
@@ -146,18 +146,19 @@
     out_ref[begin:end, cols] = (mixed[:, :HEAD] / mixed[:, HEAD : HEAD + 1]).astype(bf16)
 
 
-def average_kernel(block_rows, received_ref, average_ref, square_ref):
+def average_kernel(block_rows, received_ref, average_ref, square_hbm, square_ref, sem):
     islands, own_rows, _ = received_ref.shape
-    average = jnp.sum(received_ref[...].astype(f32), axis=0) / islands
-    average_ref[...] = average
-    squares = average * average
     lane = iota((1, 128), 1)
     row = jnp.zeros((1, 128), f32)
     for block in range(own_rows // block_rows):
-        part = squares[block * block_rows : (block + 1) * block_rows]
-        total = jnp.sum(jnp.sum(part, axis=0, keepdims=True), axis=1, keepdims=True)
+        part = slice(block * block_rows, (block + 1) * block_rows)
+        average = jnp.sum(received_ref[...].astype(f32)[:, part], axis=0) / islands
+        average_ref[part, :] = average
+        total = jnp.sum(jnp.sum(average * average, axis=0, keepdims=True), axis=1, keepdims=True)
         row = jnp.where(lane == block, total, row)
     square_ref[...] = jnp.broadcast_to(row, square_ref.shape)
+    for copy in fetch((square_ref,), (square_hbm,), sem):
+        copy.wait()
 
 
 def block_factors(square_ref, block_rows, own_rows, islands):
@@ -247,6 +248,7 @@
         shape((rows, columns), bf16),
         staged + [dma((5,))],
     )(me, owner_row, kept, global_params, local_params, residual)
+    outgoing, queries, keys, values, momentum = lax.optimization_barrier((outgoing, queries, keys, values, momentum))
     received = lax.all_to_all(
         outgoing.reshape(islands, own_rows, columns), "island", split_axis=0, concat_axis=0, tiled=True
     )
@@ -254,8 +256,9 @@
         functools.partial(average_kernel, block_rows),
         "average",
         [vmem],
-        (vmem, vmem),
+        (vmem, hbm),
         (shape((own_rows, columns), f32), shape((shards, 128), f32)),
+        [vmem((shards, 128), f32), dma((1,))],
     )(received)
     me, squares = lax.optimization_barrier((me, squares))
     squares = lax.all_to_all(squares, "mp", split_axis=0, concat_axis=0, tiled=True)

time: 67 us -> 67 us (level)
  no operation moved by 1% of the time
where the time goes in v4:
time: 67 us; the launch traced here: 66.8 us
  blocking collectives  43.2 us (64%)
  starting transfers between devices  10.7 us (16%)
  Pallas kernels  8.94 us (13%)
  waiting for transfers between devices  3.21 us (5%)
  between operations  0.73 us (1%)
    all_to_all x1, blocking collectives, local(): lax.all_to_all(outgoing.reshape(islands, own_rows, columns), 'island', sp...  24 us
    all_to_all x1, blocking collectives, local(): lax.all_to_all(fresh, 'island', split_axis=0, concat_axis=0, tiled=True)  19.2 us
    all_to_all x1, starting transfers between devices, local(): lax.all_to_all(squares, 'mp', split_axis=0, concat_axis=0, tiled=True)  10.7 us
    pallas_call x5, Pallas kernels, run(): pl.pallas_call(body, in_specs=[pl.BlockSpec(memory_space=space) for space...  8.94 us
    all_to_all x1, waiting for transfers between devices, local(): lax.all_to_all(squares, 'mp', split_axis=0, concat_axis=0, tiled=True)  3.21 us
  transfers between devices with their start and end apart: 1, of which 1 were waited for; matrix products, arithmetic and copies ran while one was open for 0% of the time, Pallas kernels for 7%

profile of v4, /device:TPU:16, one launch (start us, length us, event | category | flops | bytes accessed | tf_op | source)
XLA Modules:
  0.0 66.8 jit_solution(7865462807223938182)
XLA Ops:
  0.6 0.0 copy-start.2
  0.6 0.0 copy-start.3
  0.7 1.9 %pack.1 = bf16[512,384]{1,0:T(8,128)(2,1)S(1)} custom-call(s32[1]{0:T(128)} %bitcast.me_ref, s32[1,64]{1,0:T(1,128)} %bitcast.10, s32[16,16]{1,0:T(8,128)} %kept_hbm.3, bf16[512,384]{1,0:T(8,128)(2,1)} %global_hbm.3, bf16[512,384]{1,0:T(8,128)(2,1)} %local_hbm.3, bf16[512,384]{1,0:T(8,128)(2,1)} %residual_hbm.3), custom_call_target="tpu_custom_call" | custom-call | bytes 1048576 | tf_op jit(solution)/shard_map/pack/pallas_call | solution.py:208
  2.6 0.0 copy-start.1
  2.6 24.0 %all_to_all.21.received_ref = bf16[16,32,384]{2,1,0:T(8,128)(2,1)S(1)} all-to-all(bf16[16,32,384]{2,1,0:T(8,128)(2,1)S(1)} %bitcast.7), channel_id=1, replica_groups=mesh['island'=16,'mp'=32] {'island'}, dimensions={0} | all-to-all | bytes 786432 | tf_op jit(solution)/shard_map/all_to_all | solution.py:252
  26.5 0.8 %average.1 = (f32[32,384]{1,0:T(8,128)S(1)}, f32[32,128]{1,0:T(8,128)}) custom-call(bf16[16,32,384]{2,1,0:T(8,128)(2,1)S(1)} %all_to_all.21.received_ref), custom_call_target="tpu_custom_call" | custom-call | bytes 1048576 | tf_op jit(solution)/shard_map/average/pallas_call | solution.py:208
  27.3 10.7 %all-to-all-start.1 = ((f32[32,1,128]{2,1,0:T(1,128)}), f32[32,1,128]{2,1,0:T(1,128)S(1)}, u32[]{:S(2)}, u32[]{:S(2)}) async-start(f32[32,1,128]{2,1,0:T(1,128)} %bitcast.4), calls=%async_computation.1 | async-start | bytes 32768 | tf_op jit(solution)/shard_map/all_to_all | solution.py:264
  38.0 0.0 copy-done.2
  38.1 0.0 copy-done.3
  38.1 0.0 copy-done.1
  38.1 0.0 copy-start
  38.1 5.0 %inner.1 = (bf16[512,384]{1,0:T(8,128)(2,1)}, bf16[1024,384]{1,0:T(8,128)(2,1)}, bf16[512,512]{1,0:T(8,128)(2,1)S(1)}, bf16[32,384]{1,0:T(8,128)(2,1)S(1)}) custom-call(s32[1]{0:T(128)} %bitcast.me_ref, s32[1,64]{1,0:T(1,128)} %bitcast.11, s32[16,16]{1,0:T(8,128)} %kept_hbm.3, bf16[512,384]{1,0:T(8,128)(2,1)} %global_hbm.3, bf16[512,384]{1,0:T(8,128)(2,1)} %local_hbm.3, ...), custom_call_target="tpu_custom_call" | custom-call | flops 1207959552 | bytes 1048576 | tf_op jit(solution)/shard_map/inner/pallas_call | solution.py:208
  43.1 3.2 %all-to-all-done.1 = f32[32,1,128]{2,1,0:T(1,128)S(1)} async-done(((f32[32,1,128]{2,1,0:T(1,128)}), f32[32,1,128]{2,1,0:T(1,128)S(1)}, u32[]{:S(2)}, u32[]{:S(2)}) %all-to-all-start.1) | async-done | bytes 16416 | tf_op jit(solution)/shard_map/all_to_all | solution.py:264
  46.3 0.0 copy-done
  46.3 0.1 update.1
  46.5 19.2 %all_to_all.22.fresh_ref = bf16[16,32,384]{2,1,0:T(8,128)(2,1)S(1)} all-to-all(bf16[16,32,384]{2,1,0:T(8,128)(2,1)S(1)} %update.1), channel_id=1, replica_groups=mesh['island'=16,'mp'=32] {'island'}, dimensions={0} | all-to-all | bytes 786432 | tf_op jit(solution)/shard_map/all_to_all | solution.py:287
  65.7 1.1 %merge.1 = (f32[32,384]{1,0:T(8,128)}, bf16[512,384]{1,0:T(8,128)(2,1)}) custom-call(f32[32,128]{1,0:T(8,128)S(1)} %bitcast.9, f32[32,384]{1,0:T(8,128)S(1)} %get-tuple-element.22.average_ref, f32[32,384]{1,0:T(8,128)S(1)} %copy-done, bf16[512,512]{1,0:T(8,128)(2,1)S(1)} %get-tuple-element.28.table_ref, bf16[16,32,384]{2,1,0:T(8,128)(2,1)S(1)} %all_to_all.22.fresh_ref), custom_call_target="tpu_custom_call" | custom-call | bytes 1048576 | tf_op jit(solution)/shard_map/merge/pallas_call | solution.py:208
Async XLA Ops:
  0.6 37.4 %copy-start.2 = (bf16[1024,384]{1,0:T(8,128)(2,1)S(1)}, bf16[1024,384]{1,0:T(8,128)(2,1)}, u32[]{:S(2)}) copy-start(bf16[1024,384]{1,0:T(8,128)(2,1)} %key_ref) | copy-start | bytes 2359300
  0.6 37.4 %copy-start.3 = (bf16[1024,384]{1,0:T(8,128)(2,1)S(1)}, bf16[1024,384]{1,0:T(8,128)(2,1)}, u32[]{:S(2)}) copy-start(bf16[1024,384]{1,0:T(8,128)(2,1)} %value_ref) | copy-start | bytes 2359300
  2.6 35.5 %copy-start.1 = (bf16[1024,384]{1,0:T(8,128)(2,1)S(1)}, bf16[1024,384]{1,0:T(8,128)(2,1)}, u32[]{:S(2)}) copy-start(bf16[1024,384]{1,0:T(8,128)(2,1)} %query_ref) | copy-start | bytes 2359300
  27.3 19.0 %all-to-all-start.1 = ((f32[32,1,128]{2,1,0:T(1,128)}), f32[32,1,128]{2,1,0:T(1,128)S(1)}, u32[]{:S(2)}, u32[]{:S(2)}) async-start(f32[32,1,128]{2,1,0:T(1,128)} %bitcast.4), calls=%async_computation.1 | async-start | bytes 32768 | tf_op jit(solution)/shard_map/all_to_all | solution.py:264
  38.1 8.2 %copy-start = (f32[32,384]{1,0:T(8,128)S(1)}, f32[32,384]{1,0:T(8,128)}, u32[]{:S(2)}) copy-start(f32[32,384]{1,0:T(8,128)} %momentum_ref.1) | copy-start | bytes 147460
